TPU v7x, 32 devices: a whole 2x2x4 slice. The times are simulated.
32 devices in a mesh: grp: 4 (over x, core), wav: 8 (over z, y).
Axes of the slice: x: 2, y: 2, z: 4, core: 2. Of those that a mesh axis runs over, the one named last changes fastest.
Arguments:
- spectra: float32 [3, 8, 16, 2, 2560], P(None, 'grp', 'wav'), may hold values from -6 to 6
- legendre: float32 [16, 2560, 32], P('wav'), may hold values from -0.03125 to 0.03125
- wave_number: int32 [16], replicated, may hold values from 0 to 2559, as said below
- cycle_points: int32 [32], replicated, may hold values from 20 to 10256, as said below
- cycle_owner: int32 [64], replicated, may hold values from 0 to 63, each once
Outputs:
- grid_columns: float32 [64, 3, 8, 11264], P('grp', None, None, 'wav')
Inputs may be any that keep to these rules, and one draw needn't show every extreme that they name: `wave_number`: all distinct; entries 2 i and 2 i + 1 sum to 2559. `cycle_points`: each is 20 + 4 k for a whole k, rising with the latitude index; 20 and 10256 both occur. `cycle_owner`: A permutation of the cycles: 0 to 31 northern, 32 + i the southern mirror of latitude i.
All inputs are finite; a program needn't handle non-finite values.
Results may differ from a plain program's by a relative error of at most 0.0003.
Values sent between devices are 32-bit elements; how exact they have to be, the bound alone decides.
A program may use at most 128 MiB of HBM per device.

v0:
```python
import jax
import jax.numpy as jnp
from jax import lax
from jax.sharding import PartitionSpec as P

RMAX = 10256
TWO_PI = 6.283185307179586
HIGHEST = lax.Precision.HIGHEST


def synthesis(coeffs, wave_list, lengths, points_count):
    points = jnp.arange(points_count, dtype=jnp.int32)
    weight = jnp.where(wave_list == 0, 1.0, 2.0).astype(jnp.float32)
    wave_total = wave_list.shape[0]

    def one_cycle(cycle_args):
        cycle_block, cycle_length = cycle_args
        phases = wave_list[:, None] * points[None, :] % cycle_length
        angles = phases.astype(jnp.float32) * (TWO_PI / cycle_length.astype(jnp.float32))
        cosine = weight[:, None] * jnp.cos(angles)
        sine_part = -weight[:, None] * jnp.sin(angles)
        fourier_basis = jnp.stack([cosine, sine_part], axis=1).reshape(2 * wave_total, points_count)
        flattened = cycle_block.reshape(-1, 2 * wave_total)
        values = jnp.dot(
            flattened, fourier_basis, precision=HIGHEST, preferred_element_type=jnp.float32
        )
        values = jnp.where(points[None, :] < cycle_length, values, 0.0)
        return values.reshape(cycle_block.shape[:-1] + (points_count,))

    return lax.map(one_cycle, (coeffs, lengths))


def body(spectra, legendre, wave_number, cycle_points, cycle_owner):
    column = lax.axis_index("wav")
    wav_size = lax.axis_size("wav")
    wave_local = legendre.shape[0]
    degree_rows = legendre.shape[1]
    my_waves = lax.dynamic_slice_in_dim(wave_number, column * wave_local, wave_local)
    offsets = jnp.arange(degree_rows, dtype=jnp.int32)
    inside = my_waves[:, None] + offsets[None, :] < degree_rows
    masked = jnp.where(inside[None, None, :, None, :], spectra, 0.0)
    parity_signs = jnp.where(offsets % 2 == 0, 1.0, -1.0).astype(jnp.float32)
    mirrored = jnp.concatenate([legendre, legendre * parity_signs[None, :, None]], axis=2)
    fourier = jnp.einsum("flmck,mki->iflmc", masked, mirrored, precision=HIGHEST)
    placed = jnp.take(fourier, cycle_owner, axis=0)
    cycle_total = placed.shape[0]
    rows_first = placed.reshape(cycle_total, 3, placed.shape[2], 2 * wave_local)
    cycle_lengths = jnp.concatenate([cycle_points, cycle_points])[cycle_owner]
    segment = (RMAX + 128 * wav_size - 1) // (128 * wav_size) * 128
    owned_cycles = cycle_total // wav_size
    my_lengths = lax.dynamic_slice_in_dim(cycle_lengths, column * owned_cycles, owned_cycles)
    grid_rows = synthesis(
        lax.all_to_all(rows_first, "wav", split_axis=0, concat_axis=3, tiled=True),
        wave_number,
        my_lengths,
        segment * wav_size,
    )
    return lax.all_to_all(
        lax.all_to_all(grid_rows, "wav", split_axis=3, concat_axis=0, tiled=True),
        "grp",
        split_axis=0,
        concat_axis=2,
        tiled=True,
    )


def solution(mesh):
    in_specs = (P(None, "grp", "wav", None, None), P("wav", None, None), P(), P(), P())
    out_specs = P("grp", None, None, "wav")
    return jax.shard_map(body, mesh=mesh, in_specs=in_specs, out_specs=out_specs, check_vma=False)
```

profile of v0, /device:TPU:0, one launch (start us, length us, event | category | flops | bytes accessed | tf_op | source)
XLA Modules:
  0.0 470.3 jit_solution(11848832850669531149)
XLA Ops:
  2.2 1.1 broadcast_select_fusion
  3.3 1.1 broadcast_multiply_fusion
  4.4 2.4 fusion.16
  7.1 0.8 gather_fusion.1
  8.3 0.9 reshape.234
  9.2 7.3 %all-to-all-start = ((f32[8,1,192]{2,1,0:T(1,128)}), f32[8,1,192]{2,1,0:T(1,128)S(1)}, u32[]{:S(2)}, u32[]{:S(2)}) async-start(f32[8,1,192]{2,1,0:T(1,128)} %reshape.234), calls=%async_computation | async-start | bytes 16384 | tf_op jit(solution)/shard_map/all_to_all | solution.py:53
  17.4 5.6 %all-to-all-done = f32[8,1,192]{2,1,0:T(1,128)S(1)} async-done(((f32[8,1,192]{2,1,0:T(1,128)}), f32[8,1,192]{2,1,0:T(1,128)S(1)}, u32[]{:S(2)}, u32[]{:S(2)}) %all-to-all-start) | async-done | bytes 6176 | tf_op jit(solution)/shard_map/all_to_all | solution.py:53
  25.0 134.5 %while.13 = (s32[]{:T(128)}, f32[8,3,2,11264]{3,2,1,0:T(2,128)}, s32[8]{0:T(128)S(1)}, f32[8,3,2,32]{3,2,1,0:T(2,128)S(1)}, f32[16]{0:T(128)S(1)}, /*index=5*/s3...) while((s32[]{:T(128)}, f32[8,3,2,11264]{3,2,1,0:T(2,128)}, ...), condition=%wide.region_1.2_spmd.clone.clone, body=%wide.region_0.1_spmd.clone.clone.sunk | while | flops 28554248 | bytes 12912769 | solution.py:30
  28.4 9.6 %fusion.31 = (f32[16,1,11264]{2,0,1:T(8,128)S(1)}, f32[16,1,11264]{2,0,1:T(8,128)S(1)}) fusion(f32[]{:T(128)S(6)} %div.7, s32[]{:T(128)S(6)} %select_n.118, s32[16]{0:T(128)S(1)} %get-tuple-element.247, f32[16]{0:T(128)S(1)} %get-tuple-element.246, pred[]{:T(512)S(6)} %lt.122, f32[16]{0:T(128)S(1)} %bitcast.47), kind=kLoop, calls=%fused_computation.14.clone.1 | loop fusion | flops 2162688 | bytes 1441993 | tf_op jit(solution)/shard_map/while/body/eval_jaxpr/mul | solution.py:20
  38.1 1.1 copy.85
  39.2 1.0 reshape.241
  40.2 0.8 convolution_select_fusion.2
  45.2 9.6 %fusion.31 = (f32[16,1,11264]{2,0,1:T(8,128)S(1)}, f32[16,1,11264]{2,0,1:T(8,128)S(1)}) fusion(f32[]{:T(128)S(6)} %div.7, s32[]{:T(128)S(6)} %select_n.118, s32[16]{0:T(128)S(1)} %get-tuple-element.247, f32[16]{0:T(128)S(1)} %get-tuple-element.246, pred[]{:T(512)S(6)} %lt.122, f32[16]{0:T(128)S(1)} %bitcast.47), kind=kLoop, calls=%fused_computation.14.clone.1 | loop fusion | flops 2162688 | bytes 1441993 | tf_op jit(solution)/shard_map/while/body/eval_jaxpr/mul | solution.py:20
  54.8 1.1 copy.85
  56.0 1.0 reshape.241
  57.0 0.8 convolution_select_fusion.2
  61.9 9.6 %fusion.31 = (f32[16,1,11264]{2,0,1:T(8,128)S(1)}, f32[16,1,11264]{2,0,1:T(8,128)S(1)}) fusion(f32[]{:T(128)S(6)} %div.7, s32[]{:T(128)S(6)} %select_n.118, s32[16]{0:T(128)S(1)} %get-tuple-element.247, f32[16]{0:T(128)S(1)} %get-tuple-element.246, pred[]{:T(512)S(6)} %lt.122, f32[16]{0:T(128)S(1)} %bitcast.47), kind=kLoop, calls=%fused_computation.14.clone.1 | loop fusion | flops 2162688 | bytes 1441993 | tf_op jit(solution)/shard_map/while/body/eval_jaxpr/mul | solution.py:20
  71.6 1.1 copy.85
  72.7 1.0 reshape.241
  73.7 0.8 convolution_select_fusion.2
  78.6 9.6 %fusion.31 = (f32[16,1,11264]{2,0,1:T(8,128)S(1)}, f32[16,1,11264]{2,0,1:T(8,128)S(1)}) fusion(f32[]{:T(128)S(6)} %div.7, s32[]{:T(128)S(6)} %select_n.118, s32[16]{0:T(128)S(1)} %get-tuple-element.247, f32[16]{0:T(128)S(1)} %get-tuple-element.246, pred[]{:T(512)S(6)} %lt.122, f32[16]{0:T(128)S(1)} %bitcast.47), kind=kLoop, calls=%fused_computation.14.clone.1 | loop fusion | flops 2162688 | bytes 1441993 | tf_op jit(solution)/shard_map/while/body/eval_jaxpr/mul | solution.py:20
  88.3 1.1 copy.85
  89.4 1.0 reshape.241
  90.4 0.8 convolution_select_fusion.2
  95.4 9.6 %fusion.31 = (f32[16,1,11264]{2,0,1:T(8,128)S(1)}, f32[16,1,11264]{2,0,1:T(8,128)S(1)}) fusion(f32[]{:T(128)S(6)} %div.7, s32[]{:T(128)S(6)} %select_n.118, s32[16]{0:T(128)S(1)} %get-tuple-element.247, f32[16]{0:T(128)S(1)} %get-tuple-element.246, pred[]{:T(512)S(6)} %lt.122, f32[16]{0:T(128)S(1)} %bitcast.47), kind=kLoop, calls=%fused_computation.14.clone.1 | loop fusion | flops 2162688 | bytes 1441993 | tf_op jit(solution)/shard_map/while/body/eval_jaxpr/mul | solution.py:20
  105.1 1.1 copy.85
  106.2 1.0 reshape.241
  107.2 0.8 convolution_select_fusion.2
  112.1 9.6 %fusion.31 = (f32[16,1,11264]{2,0,1:T(8,128)S(1)}, f32[16,1,11264]{2,0,1:T(8,128)S(1)}) fusion(f32[]{:T(128)S(6)} %div.7, s32[]{:T(128)S(6)} %select_n.118, s32[16]{0:T(128)S(1)} %get-tuple-element.247, f32[16]{0:T(128)S(1)} %get-tuple-element.246, pred[]{:T(512)S(6)} %lt.122, f32[16]{0:T(128)S(1)} %bitcast.47), kind=kLoop, calls=%fused_computation.14.clone.1 | loop fusion | flops 2162688 | bytes 1441993 | tf_op jit(solution)/shard_map/while/body/eval_jaxpr/mul | solution.py:20
  121.8 1.1 copy.85
  122.9 1.0 reshape.241
  123.9 0.8 convolution_select_fusion.2
  128.9 9.6 %fusion.31 = (f32[16,1,11264]{2,0,1:T(8,128)S(1)}, f32[16,1,11264]{2,0,1:T(8,128)S(1)}) fusion(f32[]{:T(128)S(6)} %div.7, s32[]{:T(128)S(6)} %select_n.118, s32[16]{0:T(128)S(1)} %get-tuple-element.247, f32[16]{0:T(128)S(1)} %get-tuple-element.246, pred[]{:T(512)S(6)} %lt.122, f32[16]{0:T(128)S(1)} %bitcast.47), kind=kLoop, calls=%fused_computation.14.clone.1 | loop fusion | flops 2162688 | bytes 1441993 | tf_op jit(solution)/shard_map/while/body/eval_jaxpr/mul | solution.py:20
  138.5 1.1 copy.85
  139.7 1.0 reshape.241
  140.7 0.8 convolution_select_fusion.2
  145.6 9.6 %fusion.31 = (f32[16,1,11264]{2,0,1:T(8,128)S(1)}, f32[16,1,11264]{2,0,1:T(8,128)S(1)}) fusion(f32[]{:T(128)S(6)} %div.7, s32[]{:T(128)S(6)} %select_n.118, s32[16]{0:T(128)S(1)} %get-tuple-element.247, f32[16]{0:T(128)S(1)} %get-tuple-element.246, pred[]{:T(512)S(6)} %lt.122, f32[16]{0:T(128)S(1)} %bitcast.47), kind=kLoop, calls=%fused_computation.14.clone.1 | loop fusion | flops 2162688 | bytes 1441993 | tf_op jit(solution)/shard_map/while/body/eval_jaxpr/mul | solution.py:20
  155.3 1.1 copy.85
  156.4 1.0 reshape.241
  159.5 35.7 %copy.71 = f32[8,3,2,11264]{0,2,1,3:T(2,128)} copy(f32[8,3,2,11264]{3,2,1,0:T(2,128)} %get-tuple-element.78) | data formatting | bytes 4325376 | tf_op jit(solution)/shard_map/while | solution.py:30
  195.2 73.8 %reshape.236 = f32[8,1,67584]{2,1,0:T(1,128)S(1)} reshape(f32[11264,3,2,8]{3,2,1,0:T(2,128)} %bitcast.38) | data formatting | bytes 4325376
  269.0 52.3 %all_to_all.54 = f32[8,1,67584]{2,1,0:T(1,128)} all-to-all(f32[8,1,67584]{2,1,0:T(1,128)S(1)} %reshape.236), channel_id=1, replica_groups=mesh['grp'=4,'wav'=8] {'wav'}, dimensions={0} | all-to-all | bytes 4325376 | tf_op jit(solution)/shard_map/all_to_all | solution.py:59
  321.3 7.4 %reduce.1 = f32[8,67584]{1,0:T(8,128)S(1)} reduce(f32[8,1,67584]{2,1,0:T(1,128)} %all_to_all.54, f32[]{:T(128)} %broadcast.245), dimensions={1}, to_apply=%all_to_all.43.reduce_sub_computation | reduce | bytes 4325380 | tf_op jit(solution)/shard_map/all_to_all | solution.py:59
  328.7 67.0 %reshape.237 = f32[11264,3,2,8]{3,2,1,0:T(2,128)} reshape(f32[8,67584]{1,0:T(8,128)S(1)} %reduce.1) | data formatting | bytes 4325376
  395.6 41.3 %copy.81 = f32[8,3,2,8,1408]{4,0,3,2,1:T(8,128)S(1)} copy(f32[8,3,2,8,1408]{0,2,1,4,3:T(2,128)} %bitcast.39) | data formatting | bytes 4325376 | tf_op jit(solution)/shard_map/all_to_all | solution.py:59
  437.0 1.7 copy.74
  438.7 29.0 %all_to_all.55 = f32[64,3,2,1408]{3,2,1,0:T(2,128)S(1)} all-to-all(f32[64,3,2,1408]{3,2,1,0:T(2,128)S(1)} %copy.74), channel_id=1, replica_groups=mesh['grp'=4,'wav'=8] {'grp'}, dimensions={0} | all-to-all | bytes 4325376 | tf_op jit(solution)/shard_map/all_to_all | solution.py:58
  468.0 2.0 copy.77
  (84 shorter events, 24.9 us)
Async XLA Ops:
  3.2 13.2 %copy-start = (s32[16]{0:T(128)S(1)}, s32[16]{0:T(128)}, u32[]{:S(2)}) copy-start(s32[16]{0:T(128)} %param.9) | copy-start | bytes 196
  3.2 13.2 %copy-start.1 = (s32[32]{0:T(128)S(1)}, s32[32]{0:T(128)}, u32[]{:S(2)}) copy-start(s32[32]{0:T(128)} %param.10) | copy-start | bytes 388
  9.2 13.8 %all-to-all-start = ((f32[8,1,192]{2,1,0:T(1,128)}), f32[8,1,192]{2,1,0:T(1,128)S(1)}, u32[]{:S(2)}, u32[]{:S(2)}) async-start(f32[8,1,192]{2,1,0:T(1,128)} %reshape.234), calls=%async_computation | async-start | bytes 16384 | tf_op jit(solution)/shard_map/all_to_all | solution.py:53
where the time goes:
time: 478 us; the launch traced here: 470 us
  local copies, waits for them, and re-layouts  256 us (54%)
  other arithmetic  94.3 us (20%)
  blocking collectives  81.2 us (17%)
  loops' own time  16.6 us (3%)
  matrix products  8.78 us (2%)
  starting transfers between devices  7.28 us (2%)
  waiting for transfers between devices  5.56 us (1%)
    unnamed x9, local copies, waits for them, and re-layouts  142 us
    mul x8, other arithmetic, one_cycle(): cosine = weight[:, None] * jnp.cos(angles)  76.7 us
    all_to_all x1, blocking collectives, body(): lax.all_to_all(grid_rows, 'wav', split_axis=3, concat_axis=0, tiled=True)  52.3 us
    all_to_all x2, local copies, waits for them, and re-layouts, body(): lax.all_to_all(grid_rows, 'wav', split_axis=3, concat_axis=0, tiled=True)  43 us
    while x1, local copies, waits for them, and re-layouts, synthesis(): return lax.map(one_cycle, (coeffs, lengths))  35.7 us
    all_to_all x1, blocking collectives, body(): lax.all_to_all(lax.all_to_all(grid_rows, 'wav', split_axis=3, concat_axis...  29 us
    another operation x1, loops' own time, synthesis(): return lax.map(one_cycle, (coeffs, lengths))  16.6 us
  transfers between devices with their start and end apart: 1, of which 1 were waited for; matrix products, arithmetic and copies ran while one was open for 0% of the time, Pallas kernels for 0%

commit v1 on v0

--- a/solution.py
+++ b/solution.py
@@ -2,10 +2,29 @@
 import jax.numpy as jnp
 from jax import lax
 from jax.sharding import PartitionSpec as P
+from jax.lax import axis_index, ppermute, psum
 
 RMAX = 10256
 TWO_PI = 6.283185307179586
 HIGHEST = lax.Precision.HIGHEST
+
+
+def _update_rounds(in_dim, arr, d_out, axis_id):
+    arr_next = psum(1, axis_name=axis_id)
+    work_now = axis_index(axis_id)
+    outer, y_new = (arr_next, work_now)
+    aux = arr.shape[d_out] // outer
+    known = jnp.roll(arr, -y_new * aux, axis=d_out)
+    base_arr = lax.slice_in_dim(known, 0, aux, axis=d_out)
+    queue = [base_arr]
+    for p in range(1, outer):
+        vec_out = lax.slice_in_dim(known, p * aux, (p + 1) * aux, axis=d_out)
+        r1 = ppermute(
+            vec_out, axis_name=axis_id, perm=[(kk, (kk + p) % outer) for kk in range(outer)]
+        )
+        queue.append(r1)
+    parts_out = jnp.concatenate(queue[::-1], axis=in_dim)
+    return jnp.roll(parts_out, (y_new + 1) * queue[0].shape[in_dim], axis=in_dim)
 
 
 def synthesis(coeffs, wave_list, lengths, points_count):
@@ -50,10 +69,7 @@
     owned_cycles = cycle_total // wav_size
     my_lengths = lax.dynamic_slice_in_dim(cycle_lengths, column * owned_cycles, owned_cycles)
     grid_rows = synthesis(
-        lax.all_to_all(rows_first, "wav", split_axis=0, concat_axis=3, tiled=True),
-        wave_number,
-        my_lengths,
-        segment * wav_size,
+        _update_rounds(3, rows_first, 0, "wav"), wave_number, my_lengths, segment * wav_size
     )
     return lax.all_to_all(
         lax.all_to_all(grid_rows, "wav", split_axis=3, concat_axis=0, tiled=True),

time: 478 us -> 478 us (level)
  starting transfers between devices: 7.28 us -> 12.5 us
    ppermute x0 -> x7, starting transfers between devices: none -> 12.5 us  [_update_rounds(): ppermute(vec_out, axis_name=axis_id, perm=[(kk, (kk + p) % outer) for kk...]
    all_to_all x1 -> x0, starting transfers between devices: 7.28 us -> none  [body(): lax.all_to_all(rows_first, 'wav', split_axis=0, concat_axis=3, tiled=True)]
    all_to_all x1 -> x0, waiting for transfers between devices: 5.56 us -> none  [body(): lax.all_to_all(rows_first, 'wav', split_axis=0, concat_axis=3, tiled=True)]
    unnamed x9 -> x8, local copies, waits for them, and re-layouts: 142 us -> 141 us
    all_to_all x2 -> x3, local copies, waits for them, and re-layouts: 43 us -> 43.5 us  [body(): lax.all_to_all(grid_rows, 'wav', split_axis=3, concat_axis=0, tiled=True)]
  transfers between devices with their start and end apart: 1 -> 7, of which waited for: 1 -> 3; matrix products, arithmetic and copies ran while one was open for 0% -> 0% of each run, Pallas kernels for 0% -> 0%
where the time goes in v1:
time: 478 us; the launch traced here: 470 us
  local copies, waits for them, and re-layouts  255 us (53%)
  other arithmetic  92.4 us (19%)
  blocking collectives  79.9 us (17%)
  loops' own time  16.6 us (3%)
  starting transfers between devices  12.5 us (3%)
  matrix products  8.78 us (2%)
    unnamed x8, local copies, waits for them, and re-layouts  141 us
    mul x8, other arithmetic, one_cycle(): cosine = weight[:, None] * jnp.cos(angles)  76.6 us
    all_to_all x1, blocking collectives, body(): lax.all_to_all(grid_rows, 'wav', split_axis=3, concat_axis=0, tiled=True)  50.9 us
    all_to_all x3, local copies, waits for them, and re-layouts, body(): lax.all_to_all(grid_rows, 'wav', split_axis=3, concat_axis=0, tiled=True)  43.5 us
    while x1, local copies, waits for them, and re-layouts, synthesis(): return lax.map(one_cycle, (coeffs, lengths))  35.7 us
    all_to_all x1, blocking collectives, body(): lax.all_to_all(lax.all_to_all(grid_rows, 'wav', split_axis=3, concat_axis...  29 us
    another operation x1, loops' own time, synthesis(): return lax.map(one_cycle, (coeffs, lengths))  16.6 us
    ppermute x7, starting transfers between devices, _update_rounds(): ppermute(vec_out, axis_name=axis_id, perm=[(kk, (kk + p) % outer) for kk...  12.5 us
  transfers between devices with their start and end apart: 7, of which 3 were waited for; matrix products, arithmetic and copies ran while one was open for 0% of the time, Pallas kernels for 0%

profile of v1, /device:TPU:0, one launch (start us, length us, event | category | flops | bytes accessed | tf_op | source)
XLA Modules:
  0.0 469.9 jit_solution(13260142557726816903)
XLA Ops:
  0.9 1.1 broadcast_select_fusion
  1.9 1.1 broadcast_multiply_fusion
  3.1 2.4 fusion.16
  5.9 0.8 gather_fusion.1
  7.1 6.1 %collective-permute-start = (f32[8,3,2,4]{0,3,2,1:T(4,128)S(1)}, f32[8,3,2,4]{0,3,2,1:T(4,128)S(1)}, u32[]{:S(2)}, u32[]{:S(2)}) collective-permute-start(f32[8,3,2,4]{0,3,2,1:T(4,128)S(1)} %get-tuple-element.180), channel_id=1, source_target_pairs={{0,7},{1,0},{2,1},{3,2},{4,3},{5,4},{6,5},{7,6},{8,15},{9,8},{10,9... | collective-permute-start | bytes 2312 | tf_op jit(solution)/shard_map/ppermute | solution.py:22
  13.6 3.0 collective-permute-start.3
  16.7 1.9 collective-permute-start.5
  18.6 1.1 collective-permute-start.6
  21.0 1.1 collective-permute-done.4
  22.2 1.0 collective-permute-done.5
  23.3 1.7 collective-permute-done.6
  25.3 134.4 %while.13 = (s32[]{:T(128)}, f32[8,3,2,11264]{3,2,1,0:T(2,128)}, s32[8]{0:T(128)S(1)}, f32[8,3,2,32]{3,0,2,1:T(8,128)S(1)}, f32[16]{0:T(128)S(1)}, /*index=5*/s3...) while((s32[]{:T(128)}, f32[8,3,2,11264]{3,2,1,0:T(2,128)}, ...), condition=%wide.region_1.2_spmd.clone.clone, body=%wide.region_0.1_spmd.clone.clone.sunk | while | flops 28554248 | bytes 12913269 | solution.py:49
  28.1 9.6 %fusion.32 = (f32[16,1,11264]{2,0,1:T(8,128)S(1)}, f32[16,1,11264]{2,0,1:T(8,128)S(1)}) fusion(f32[]{:T(128)S(6)} %div.7, s32[]{:T(128)S(6)} %select_n.144, s32[16]{0:T(128)S(1)} %get-tuple-element.257, f32[16]{0:T(128)S(1)} %get-tuple-element.256, pred[]{:T(512)S(6)} %lt.148, f32[16]{0:T(128)S(1)} %bitcast.45), kind=kLoop, calls=%fused_computation.14.clone.1 | loop fusion | flops 2162688 | bytes 1441993 | tf_op jit(solution)/shard_map/while/body/eval_jaxpr/mul | solution.py:39
  37.8 1.1 copy.135
  38.9 1.0 reshape.239
  40.6 0.8 convolution_select_fusion.2
  44.8 9.6 %fusion.32 = (f32[16,1,11264]{2,0,1:T(8,128)S(1)}, f32[16,1,11264]{2,0,1:T(8,128)S(1)}) fusion(f32[]{:T(128)S(6)} %div.7, s32[]{:T(128)S(6)} %select_n.144, s32[16]{0:T(128)S(1)} %get-tuple-element.257, f32[16]{0:T(128)S(1)} %get-tuple-element.256, pred[]{:T(512)S(6)} %lt.148, f32[16]{0:T(128)S(1)} %bitcast.45), kind=kLoop, calls=%fused_computation.14.clone.1 | loop fusion | flops 2162688 | bytes 1441993 | tf_op jit(solution)/shard_map/while/body/eval_jaxpr/mul | solution.py:39
  54.5 1.1 copy.135
  55.6 1.0 reshape.239
  61.5 9.6 %fusion.32 = (f32[16,1,11264]{2,0,1:T(8,128)S(1)}, f32[16,1,11264]{2,0,1:T(8,128)S(1)}) fusion(f32[]{:T(128)S(6)} %div.7, s32[]{:T(128)S(6)} %select_n.144, s32[16]{0:T(128)S(1)} %get-tuple-element.257, f32[16]{0:T(128)S(1)} %get-tuple-element.256, pred[]{:T(512)S(6)} %lt.148, f32[16]{0:T(128)S(1)} %bitcast.45), kind=kLoop, calls=%fused_computation.14.clone.1 | loop fusion | flops 2162688 | bytes 1441993 | tf_op jit(solution)/shard_map/while/body/eval_jaxpr/mul | solution.py:39
  71.2 1.1 copy.135
  72.3 1.0 reshape.239
  78.3 9.6 %fusion.32 = (f32[16,1,11264]{2,0,1:T(8,128)S(1)}, f32[16,1,11264]{2,0,1:T(8,128)S(1)}) fusion(f32[]{:T(128)S(6)} %div.7, s32[]{:T(128)S(6)} %select_n.144, s32[16]{0:T(128)S(1)} %get-tuple-element.257, f32[16]{0:T(128)S(1)} %get-tuple-element.256, pred[]{:T(512)S(6)} %lt.148, f32[16]{0:T(128)S(1)} %bitcast.45), kind=kLoop, calls=%fused_computation.14.clone.1 | loop fusion | flops 2162688 | bytes 1441993 | tf_op jit(solution)/shard_map/while/body/eval_jaxpr/mul | solution.py:39
  88.0 1.1 copy.135
  89.1 1.0 reshape.239
  95.0 9.6 %fusion.32 = (f32[16,1,11264]{2,0,1:T(8,128)S(1)}, f32[16,1,11264]{2,0,1:T(8,128)S(1)}) fusion(f32[]{:T(128)S(6)} %div.7, s32[]{:T(128)S(6)} %select_n.144, s32[16]{0:T(128)S(1)} %get-tuple-element.257, f32[16]{0:T(128)S(1)} %get-tuple-element.256, pred[]{:T(512)S(6)} %lt.148, f32[16]{0:T(128)S(1)} %bitcast.45), kind=kLoop, calls=%fused_computation.14.clone.1 | loop fusion | flops 2162688 | bytes 1441993 | tf_op jit(solution)/shard_map/while/body/eval_jaxpr/mul | solution.py:39
  104.7 1.1 copy.135
  105.8 1.0 reshape.239
  111.7 9.6 %fusion.32 = (f32[16,1,11264]{2,0,1:T(8,128)S(1)}, f32[16,1,11264]{2,0,1:T(8,128)S(1)}) fusion(f32[]{:T(128)S(6)} %div.7, s32[]{:T(128)S(6)} %select_n.144, s32[16]{0:T(128)S(1)} %get-tuple-element.257, f32[16]{0:T(128)S(1)} %get-tuple-element.256, pred[]{:T(512)S(6)} %lt.148, f32[16]{0:T(128)S(1)} %bitcast.45), kind=kLoop, calls=%fused_computation.14.clone.1 | loop fusion | flops 2162688 | bytes 1441993 | tf_op jit(solution)/shard_map/while/body/eval_jaxpr/mul | solution.py:39
  121.4 1.1 copy.135
  122.6 1.0 reshape.239
  124.2 0.8 convolution_select_fusion.2
  128.5 9.6 %fusion.32 = (f32[16,1,11264]{2,0,1:T(8,128)S(1)}, f32[16,1,11264]{2,0,1:T(8,128)S(1)}) fusion(f32[]{:T(128)S(6)} %div.7, s32[]{:T(128)S(6)} %select_n.144, s32[16]{0:T(128)S(1)} %get-tuple-element.257, f32[16]{0:T(128)S(1)} %get-tuple-element.256, pred[]{:T(512)S(6)} %lt.148, f32[16]{0:T(128)S(1)} %bitcast.45), kind=kLoop, calls=%fused_computation.14.clone.1 | loop fusion | flops 2162688 | bytes 1441993 | tf_op jit(solution)/shard_map/while/body/eval_jaxpr/mul | solution.py:39
  138.2 1.1 copy.135
  139.3 1.0 reshape.239
  145.2 9.6 %fusion.32 = (f32[16,1,11264]{2,0,1:T(8,128)S(1)}, f32[16,1,11264]{2,0,1:T(8,128)S(1)}) fusion(f32[]{:T(128)S(6)} %div.7, s32[]{:T(128)S(6)} %select_n.144, s32[16]{0:T(128)S(1)} %get-tuple-element.257, f32[16]{0:T(128)S(1)} %get-tuple-element.256, pred[]{:T(512)S(6)} %lt.148, f32[16]{0:T(128)S(1)} %bitcast.45), kind=kLoop, calls=%fused_computation.14.clone.1 | loop fusion | flops 2162688 | bytes 1441993 | tf_op jit(solution)/shard_map/while/body/eval_jaxpr/mul | solution.py:39
  154.9 1.1 copy.135
  156.0 1.0 reshape.239
  157.7 0.8 convolution_select_fusion.2
  159.8 35.7 %copy.121 = f32[8,3,2,11264]{0,2,1,3:T(2,128)} copy(f32[8,3,2,11264]{3,2,1,0:T(2,128)} %get-tuple-element.78) | data formatting | bytes 4325376 | tf_op jit(solution)/shard_map/while | solution.py:49
  195.5 73.8 %reshape.234 = f32[8,1,67584]{2,1,0:T(1,128)S(1)} reshape(f32[11264,3,2,8]{3,2,1,0:T(2,128)} %bitcast.38) | data formatting | bytes 4325376
  269.3 50.9 %all_to_all.36 = f32[8,1,67584]{2,1,0:T(1,128)} all-to-all(f32[8,1,67584]{2,1,0:T(1,128)S(1)} %reshape.234), channel_id=1, replica_groups=mesh['grp'=4,'wav'=8] {'wav'}, dimensions={0} | all-to-all | bytes 4325376 | tf_op jit(solution)/shard_map/all_to_all | solution.py:75
  320.8 7.4 %reduce = f32[8,67584]{1,0:T(8,128)S(1)} reduce(f32[8,1,67584]{2,1,0:T(1,128)} %all_to_all.36, f32[]{:T(128)} %broadcast.247), dimensions={1}, to_apply=%all_to_all.26.reduce_sub_computation | reduce | bytes 4325380 | tf_op jit(solution)/shard_map/all_to_all | solution.py:75
  328.2 67.1 %reshape.235 = f32[11264,3,2,8]{3,2,1,0:T(2,128)} reshape(f32[8,67584]{1,0:T(8,128)S(1)} %reduce) | data formatting | bytes 4325376
  395.3 41.3 %copy.130 = f32[8,3,2,8,1408]{4,0,3,2,1:T(8,128)S(1)} copy(f32[8,3,2,8,1408]{0,2,1,4,3:T(2,128)} %bitcast.39) | data formatting | bytes 4325376 | tf_op jit(solution)/shard_map/all_to_all | solution.py:75
  436.6 1.7 copy.124
  438.3 29.0 %all_to_all.37 = f32[64,3,2,1408]{3,2,1,0:T(2,128)S(1)} all-to-all(f32[64,3,2,1408]{3,2,1,0:T(2,128)S(1)} %copy.124), channel_id=1, replica_groups=mesh['grp'=4,'wav'=8] {'grp'}, dimensions={0} | all-to-all | bytes 4325376 | tf_op jit(solution)/shard_map/all_to_all | solution.py:74
  467.7 2.0 copy.127
  (102 shorter events, 26.8 us)
Async XLA Ops:
  0.0 5.8 %copy-start.1 = (s32[64]{0:T(128)S(1)}, s32[64]{0:T(128)}, u32[]{:S(2)}) copy-start(s32[64]{0:T(128)} %param.11) | copy-start | bytes 772
  0.0 5.8 %copy-start.2 = (s32[32]{0:T(128)S(1)}, s32[32]{0:T(128)}, u32[]{:S(2)}) copy-start(s32[32]{0:T(128)} %param.10) | copy-start | bytes 388
  1.9 14.7 %copy-start = (s32[16]{0:T(128)S(1)}, s32[16]{0:T(128)}, u32[]{:S(2)}) copy-start(s32[16]{0:T(128)} %param.9) | copy-start | bytes 196
  7.1 9.6 %collective-permute-start = (f32[8,3,2,4]{0,3,2,1:T(4,128)S(1)}, f32[8,3,2,4]{0,3,2,1:T(4,128)S(1)}, u32[]{:S(2)}, u32[]{:S(2)}) collective-permute-start(f32[8,3,2,4]{0,3,2,1:T(4,128)S(1)} %get-tuple-element.180), channel_id=1, source_target_pairs={{0,7},{1,0},{2,1},{3,2},{4,3},{5,4},{6,5},{7,6},{8,15},{9,8},{10,9... | collective-permute-start | bytes 2312 | tf_op jit(solution)/shard_map/ppermute | solution.py:22
  13.1 5.4 %collective-permute-start.1 = (f32[8,3,2,4]{0,3,2,1:T(4,128)S(1)}, f32[8,3,2,4]{0,3,2,1:T(4,128)S(1)}, u32[]{:S(2)}, u32[]{:S(2)}) collective-permute-start(f32[8,3,2,4]{0,3,2,1:T(4,128)S(1)} %get-tuple-element.179), channel_id=1, source_target_pairs={{0,6},{1,7},{2,0},{3,1},{4,2},{5,3},{6,4},{7,5},{8,14},{9,15},{10,... | collective-permute-start | bytes 2312 | tf_op jit(solution)/shard_map/ppermute | solution.py:22
  13.6 7.2 %collective-permute-start.2 = (f32[8,3,2,4]{0,3,2,1:T(4,128)S(1)}, f32[8,3,2,4]{0,3,2,1:T(4,128)S(1)}, u32[]{:S(2)}, u32[]{:S(2)}) collective-permute-start(f32[8,3,2,4]{0,3,2,1:T(4,128)S(1)} %get-tuple-element.178), channel_id=1, source_target_pairs={{0,5},{1,6},{2,7},{3,0},{4,1},{5,2},{6,3},{7,4},{8,13},{9,14},{10,... | collective-permute-start | bytes 2312 | tf_op jit(solution)/shard_map/ppermute | solution.py:22
  13.6 7.3 %collective-permute-start.3 = (f32[8,3,2,4]{0,3,2,1:T(4,128)S(1)}, f32[8,3,2,4]{0,3,2,1:T(4,128)S(1)}, u32[]{:S(2)}, u32[]{:S(2)}) collective-permute-start(f32[8,3,2,4]{0,3,2,1:T(4,128)S(1)} %get-tuple-element.177), channel_id=1, source_target_pairs={{0,4},{1,5},{2,6},{3,7},{4,0},{5,1},{6,2},{7,3},{8,12},{9,13},{10,... | collective-permute-start | bytes 2312 | tf_op jit(solution)/shard_map/ppermute | solution.py:22
  16.6 5.5 %collective-permute-start.4 = (f32[8,3,2,4]{0,3,2,1:T(4,128)S(1)}, f32[8,3,2,4]{0,3,2,1:T(4,128)S(1)}, u32[]{:S(2)}, u32[]{:S(2)}) collective-permute-start(f32[8,3,2,4]{0,3,2,1:T(4,128)S(1)} %get-tuple-element.176), channel_id=1, source_target_pairs={{0,3},{1,4},{2,5},{3,6},{4,7},{5,0},{6,1},{7,2},{8,11},{9,12},{10,... | collective-permute-start | bytes 2312 | tf_op jit(solution)/shard_map/ppermute | solution.py:22
  16.7 6.5 %collective-permute-start.5 = (f32[8,3,2,4]{0,3,2,1:T(4,128)S(1)}, f32[8,3,2,4]{0,3,2,1:T(4,128)S(1)}, u32[]{:S(2)}, u32[]{:S(2)}) collective-permute-start(f32[8,3,2,4]{0,3,2,1:T(4,128)S(1)} %get-tuple-element.175), channel_id=1, source_target_pairs={{0,2},{1,3},{2,4},{3,5},{4,6},{5,7},{6,0},{7,1},{8,10},{9,11},{10,... | collective-permute-start | bytes 2312 | tf_op jit(solution)/shard_map/ppermute | solution.py:22
  18.6 6.4 %collective-permute-start.6 = (f32[8,3,2,4]{0,3,2,1:T(4,128)S(1)}, f32[8,3,2,4]{0,3,2,1:T(4,128)S(1)}, u32[]{:S(2)}, u32[]{:S(2)}) collective-permute-start(f32[8,3,2,4]{0,3,2,1:T(4,128)S(1)} %get-tuple-element.174), channel_id=1, source_target_pairs={{0,1},{1,2},{2,3},{3,4},{4,5},{5,6},{6,7},{7,0},{8,9},{9,10},{10,1... | collective-permute-start | bytes 2312 | tf_op jit(solution)/shard_map/ppermute | solution.py:22
